TPU v7x, 256 devices: a whole 4x4x8 slice. The times are simulated.
256 devices in a mesh: context: 16 (over z_lo, x), tensor: 16 (over z_hi, y, core).
Axes of the slice: x: 4, y: 4, z: 8 (z_hi: 2, z_lo: 4; z = z_hi * 4 + z_lo), core: 2. Of those that a mesh axis runs over, the one named last changes fastest.
Arguments:
- tokens: bfloat16 [32768, 4096], P(('context', 'tensor')), may hold values from -6 to 6
- norm_gain: bfloat16 [4096], replicated, may hold values from 0.5 to 1.5
- in_weight: bfloat16 [4096, 3, 4096], P(None, None, 'tensor'), may hold values from -0.09375 to 0.09375
- short_filter: bfloat16 [3, 3, 4096], P(None, None, 'tensor'), may hold values from -3.5 to 3.5
- long_filter: bfloat16 [256, 128], P('tensor'), may hold values from -0.5 to 0.5
- doc_start: int32 [32768], P('context'), may hold values from 0 to 32767, as said below
Outputs:
- layer_out: bfloat16 [32768, 4096], P(('context', 'tensor'))
Inputs may be any that keep to these rules, and one draw needn't show every extreme that they name: doc_start[0] = 0, and for t > 0 doc_start[t] is either doc_start[t - 1] or t, so documents are contiguous runs of positions; the last position begins a document.
All inputs are finite; a program needn't handle non-finite values.
Results may differ from a plain program's by a relative error of at most 0.0089.
Values may be sent and summed in bfloat16 or wider, within the bound.
No kernel may reach another device: no remote copies, remote signals or barrier semaphores. Data moves between devices by JAX's collectives and lax.ppermute only.
A program may use at most 128 MiB of HBM per device.

v0:
```python
import jax
import jax.numpy as jnp
from jax import lax
from jax.sharding import PartitionSpec as P


def from_behind(shard, axis, by):
    size = lax.axis_size(axis)
    pairs = [(i, i + by) for i in range(size) if 0 <= i + by < size]
    return lax.ppermute(shard, axis, pairs)


def banded(long_filter, span):
    groups = long_filter.shape[0]
    reversed_pad = jnp.concatenate(
        [long_filter[:, ::-1], jnp.zeros((groups, span), long_filter.dtype)], axis=1
    )
    tiled = jnp.tile(reversed_pad, (1, span))[:, : span * (2 * span - 1)]
    return tiled.reshape(groups, span, 2 * span - 1)


def short_mix(padded, positions, starts, filters):
    out_count = positions.shape[0]
    short_taps = filters.shape[1]
    summed = jnp.zeros((out_count,) + padded.shape[1:], jnp.float32)
    for lag_step in range(short_taps):
        begin = short_taps - 1 - lag_step
        rows_in = lax.slice_in_dim(padded, begin, begin + out_count, axis=0).astype(jnp.float32)
        kept_mask = (positions - lag_step >= starts)[:, None, None]
        summed = summed + jnp.where(
            kept_mask, filters[:, lag_step, :].astype(jnp.float32)[None] * rows_in, 0.0
        )
    return summed


def per_device(tokens, norm_gain, in_weight, short_filter, long_filter, doc_start):
    width = tokens.shape[1]
    channels = in_weight.shape[2]
    groups = long_filter.shape[0]
    span = long_filter.shape[1]
    share = channels // groups
    short_taps = short_filter.shape[1]
    float_tokens = tokens.astype(jnp.float32)
    scale_rows = lax.rsqrt(jnp.mean(float_tokens * float_tokens, axis=-1, keepdims=True) + 1e-06)
    normed = (float_tokens * scale_rows * norm_gain.astype(jnp.float32)[None]).astype(jnp.bfloat16)
    flat_weight = in_weight.reshape(width, 3 * channels)
    projected = jnp.dot(
        lax.all_gather(normed, "tensor", axis=0, tiled=True),
        flat_weight,
        preferred_element_type=jnp.float32,
    ).astype(jnp.bfloat16)
    length = projected.shape[0]
    projected = projected.reshape(length, 3, channels)
    starts = doc_start - lax.axis_index("context") * length
    local_rows = jnp.arange(length, dtype=jnp.int32)
    rim_rows = from_behind(projected[length - (short_taps - 1) :], "context", 1)
    padded = jnp.concatenate([rim_rows, projected], axis=0)
    mixed = short_mix(padded, local_rows, starts, short_filter)
    key_value = (mixed[:, 1] * mixed[:, 2]).astype(jnp.bfloat16)
    tail_rows = from_behind(key_value[length - (span - 1) :], "context", 1)
    query = mixed[:, 0]
    extended = jnp.concatenate([tail_rows, key_value], axis=0)
    blocks = length // span
    head_part = extended[:length].reshape(blocks, span, channels)
    rest_part = jnp.concatenate([extended[span:], jnp.zeros((1, channels), jnp.bfloat16)], axis=0)
    rest_part = rest_part.reshape(blocks, span, channels)[:, : span - 1]
    window = jnp.concatenate([head_part, rest_part], axis=1).reshape(
        blocks, 2 * span - 1, groups, share
    )
    inputs = (
        (jnp.arange(blocks, dtype=jnp.int32) * span)[:, None]
        + jnp.arange(2 * span - 1, dtype=jnp.int32)[None]
        - (span - 1)
    )
    block_starts = starts.reshape(blocks, span)
    kept_mask = inputs[:, None, :] >= block_starts[:, :, None]
    toeplitz = banded(long_filter, span)
    weights = jnp.where(kept_mask[:, None], toeplitz[None], jnp.zeros((), jnp.bfloat16))
    conv = jnp.einsum(
        "bgij,bjgc->bigc", weights, window, preferred_element_type=jnp.float32
    ).reshape(length, channels)
    gated = (query * conv).astype(jnp.bfloat16)
    returned = lax.all_to_all(gated, "tensor", split_axis=0, concat_axis=1, tiled=True)
    return (float_tokens + returned.astype(jnp.float32)).astype(jnp.bfloat16)


def solution(mesh):
    in_specs = (
        P(("context", "tensor"), None),
        P(),
        P(None, None, "tensor"),
        P(None, None, "tensor"),
        P("tensor", None),
        P("context"),
    )
    out_specs = P(("context", "tensor"), None)
    return jax.shard_map(
        per_device, mesh=mesh, in_specs=in_specs, out_specs=out_specs, check_vma=False
    )
```

profile of v0, /device:TPU:70, one launch (start us, length us, event | category | flops | bytes accessed | tf_op | source)
XLA Modules:
  0.0 295.7 jit_solution(7310383108310972181)
XLA Ops:
  7.2 1.5 fusion.6
  8.8 2.5 fusion.8
  11.3 8.8 %copy.11 = bf16[4096,3,256]{0,2,1:T(8,128)(2,1)} copy(bf16[4096,3,256]{2,0,1:T(8,128)(2,1)} %param.8) | data formatting | bytes 12582912 | tf_op args[2]
  21.4 163.9 %all-gather.2.cloned.1.call-done = bf16[2048,4096]{1,0:T(8,128)(2,1)} async-done(((bf16[128,4096]{1,0:T(8,128)(2,1)}), bf16[2048,4096]{1,0:T(8,128)(2,1)}) %all-gather.2.cloned.1.call-update) | async-done | bytes 16777232 | tf_op jit(solution)/shard_map/all_gather | solution.py:48
  185.3 18.2 %convolution_convert_fusion = bf16[2048,768]{1,0:T(8,128)(2,1)S(1)} fusion(bf16[2048,4096]{1,0:T(8,128)(2,1)} %all-gather.2.cloned.1.call-done, bf16[4096,768]{0,1:T(8,128)(2,1)} %bitcast.46), kind=kOutput, calls=%fused_computation.6 | convolution fusion | flops 12886474752 | bytes 26214400 | tf_op jit(solution)/shard_map/dot_general | solution.py:47
  203.5 1.6 copy-done.1
  205.3 1.9 collective-permute-start
  208.4 3.2 %copy.12 = bf16[2048,768]{0,1:T(8,128)(2,1)S(1)} copy(bf16[2048,768]{1,0:T(8,128)(2,1)} %copy-done.1) | data formatting | bytes 6291456 | tf_op jit(solution)/shard_map/convert_element_type | solution.py:51
  211.6 2.6 collective-permute-done
  214.2 5.0 %select_add_fusion = f32[2048,3,256]{0,2,1:T(8,128)S(1)} fusion(bf16[2048,3,256]{0,2,1:T(8,128)(2,1)S(1)} %bitcast.43, bf16[2,3,256]{0,2,1:T(8,128)(2,1)S(1)} %collective-permute-done, f32[3,256]{1,0:T(4,128)} %get-tuple-element.13, f32[3,256]{1,0:T(4,128)} %get-tuple-element.14, f32[3,256]{1,0:T(4,128)} %bitcast.56, pred[2048]{0:T(1024)(128)(4,1)} %get-tuple-element.9, ...), kind=kLoop, calls=%fused_computation.5 | loop fusion | flops 26738688 | bytes 9455616 | tf_op jit(solution)/shard_map/add | solution.py:30
  219.3 1.9 slice_bitcast_fusion
  221.2 4.5 %collective-permute-start.1 = (bf16[127,256]{0,1:T(8,128)(2,1)S(1)}, bf16[127,256]{0,1:T(8,128)(2,1)S(1)}, u32[]{:S(2)}, u32[]{:S(2)}) collective-permute-start(bf16[127,256]{0,1:T(8,128)(2,1)S(1)} %slice_bitcast_fusion.1), channel_id=1, source_target_pairs={{0,16},{16,32},{32,48},{48,64},{64,80},{80,96},{96,112},{112,128},... | collective-permute-start | bytes 195080 | tf_op jit(solution)/shard_map/ppermute | solution.py:10
  225.7 1.2 broadcast_compare_fusion
  227.7 4.3 %broadcast_in_dim.65 = bf16[16,128,255]{2,1,0:T(8,128)(2,1)} reshape(bf16[16,32640]{1,0:T(8,128)(2,1)S(1)} %slice.77) | data formatting | bytes 2088960 | tf_op jit(solution)/shard_map/jit(_where)/broadcast_in_dim | solution.py:78
  233.6 1.4 copy.27
  235.0 2.0 copy.28
  237.1 1.2 pad_maximum_fusion.1
  238.3 1.5 copy.16
  240.4 0.7 copy-done.2
  241.1 5.8 %fusion = f32[16,16,16,128]{3,2,1,0:T(8,128)S(1)} fusion(pred[16,128,255]{2,1,0:T(8,128)(4,1)} %broadcast_compare_fusion, bf16[16,128,255]{2,1,0:T(8,128)(2,1)S(1)} %copy-done.2, bf16[16,127,16,16]{1,3,2,0:T(8,128)(2,1)} %bitcast.54, bf16[16,128,16,16]{1,3,2,0:T(8,128)(2,1)S(1)} %copy.19), kind=kOutput, calls=%fused_computation | convolution fusion | flops 279920640 | bytes 5752832 | tf_op jit(solution)/shard_map/bgij,bjgc->bigc/dot_general | solution.py:79
  246.9 0.7 fusion.14
  247.6 36.4 %all_to_all.10 = bf16[16,128,256]{1,2,0:T(8,128)(2,1)S(1)} all-to-all(bf16[16,128,256]{1,2,0:T(8,128)(2,1)S(1)} %fusion.14), channel_id=1, replica_groups=mesh['context'=16,'tensor'=16] {'tensor'}, dimensions={0} | all-to-all | bytes 2097152 | tf_op jit(solution)/shard_map/all_to_all | solution.py:83
  284.2 1.8 copy.23
  286.0 2.8 fusion.9
  (40 shorter events, 6.7 us)
Async XLA Ops:
  6.5 178.7 %all-gather.2.cloned.1.call-start = ((), (), s32[]{:S(2)}) async-start(), calls=%async_computation.1 | async-start | bytes 17825792 | tf_op jit(solution)/shard_map/all_gather | solution.py:48
  11.3 8.8 %copy-start.5 = (bf16[3,3,256]{2,1,0:T(4,128)(2,1)S(1)}, bf16[3,3,256]{2,1,0:T(4,128)(2,1)}, u32[]{:S(2)}) copy-start(bf16[3,3,256]{2,1,0:T(4,128)(2,1)} %param.9) | copy-start | bytes 13828
  11.3 9.4 %copy-start.4 = (s32[2048]{0:T(1024)S(1)}, s32[2048]{0:T(1024)}, u32[]{:S(2)}) copy-start(s32[2048]{0:T(1024)} %param.11) | copy-start | bytes 24580
  203.5 1.6 copy-start.1
  205.3 9.0 %collective-permute-start = (bf16[2,3,256]{0,2,1:T(8,128)(2,1)S(1)}, bf16[2,3,256]{0,2,1:T(8,128)(2,1)S(1)}, u32[]{:S(2)}, u32[]{:S(2)}) collective-permute-start(bf16[2,3,256]{0,2,1:T(8,128)(2,1)S(1)} %bitcast.55), channel_id=1, source_target_pairs={{0,16},{16,32},{32,48},{48,64},{64,80},{80,96},{96,112},{112,128},... | collective-permute-start | bytes 9224 | tf_op jit(solution)/shard_map/ppermute | solution.py:10
  219.2 6.5 %copy-start.3 = (s32[16,128]{1,0:T(8,128)S(1)}, s32[16,128]{1,0:T(8,128)}, u32[]{:S(2)}) copy-start(s32[16,128]{1,0:T(8,128)} %subtract_bitcast_fusion) | copy-start | bytes 24580
  219.2 7.6 %copy-start.6 = (bf16[16,128]{1,0:T(8,128)(2,1)S(1)}, bf16[16,128]{1,0:T(8,128)(2,1)}, u32[]{:S(2)}) copy-start(bf16[16,128]{1,0:T(8,128)(2,1)} %param.10) | copy-start | bytes 12292
  221.2 15.8 %collective-permute-start.1 = (bf16[127,256]{0,1:T(8,128)(2,1)S(1)}, bf16[127,256]{0,1:T(8,128)(2,1)S(1)}, u32[]{:S(2)}, u32[]{:S(2)}) collective-permute-start(bf16[127,256]{0,1:T(8,128)(2,1)S(1)} %slice_bitcast_fusion.1), channel_id=1, source_target_pairs={{0,16},{16,32},{32,48},{48,64},{64,80},{80,96},{96,112},{112,128},... | collective-permute-start | bytes 195080 | tf_op jit(solution)/shard_map/ppermute | solution.py:10
  239.8 1.2 copy-start.2
  284.0 2.0 copy-start
Sparse Core Ops, SparseCore 0:
  11.4 173.7 all-gather.1
where the time goes:
time: 296 us
  waiting for transfers between devices  167 us (56%)
  blocking collectives  36.4 us (12%)
  local copies, waits for them, and re-layouts  29.7 us (10%)
  matrix products  24 us (8%)
  other arithmetic  19 us (6%)
  between operations  13.6 us (5%)
  starting transfers between devices  6.41 us (2%)
    all_gather x1, waiting for transfers between devices, per_device(): lax.all_gather(normed, 'tensor', axis=0, tiled=True)  164 us
    all_to_all x1, blocking collectives, per_device(): lax.all_to_all(gated, 'tensor', split_axis=0, concat_axis=1, tiled=True)  36.4 us
    dot_general x1, matrix products, per_device(): jnp.dot(lax.all_gather(normed, 'tensor', axis=0, tiled=True), flat_weight...  18.2 us
    unnamed x21, local copies, waits for them, and re-layouts  16.5 us
    ppermute x2, starting transfers between devices, from_behind(): return lax.ppermute(shard, axis, pairs)  6.41 us
  transfers between devices with their start and end apart: 3, of which 2 were waited for; matrix products, arithmetic and copies ran while one was open for 9% of the time, Pallas kernels for 0%

commit v1 on v0

--- a/solution.py
+++ b/solution.py
@@ -45,7 +45,9 @@
     normed = (float_tokens * scale_rows * norm_gain.astype(jnp.float32)[None]).astype(jnp.bfloat16)
     flat_weight = in_weight.reshape(width, 3 * channels)
     projected = jnp.dot(
-        lax.all_gather(normed, "tensor", axis=0, tiled=True),
+        jnp.concatenate(
+            lax.all_to_all(jnp.stack([normed] * lax.axis_size("tensor")), "tensor", 0, 0), axis=0
+        ),
         flat_weight,
         preferred_element_type=jnp.float32,
     ).astype(jnp.bfloat16)

time: 296 us -> 612 us (2.07)
  waiting for transfers between devices: 167 us -> 473 us
  between operations: 13.6 us -> 0.24 us
  starting transfers between devices: 6.41 us -> 18.1 us
    all_to_all x0 -> x1, waiting for transfers between devices: none -> 462 us  [per_device(): lax.all_to_all(jnp.stack([normed] * lax.axis_size('tensor')), 'tensor', 0...]
    all_gather x1 -> x0, waiting for transfers between devices: 164 us -> none  [per_device(): lax.all_gather(normed, 'tensor', axis=0, tiled=True)]
    all_to_all x0 -> x1, starting transfers between devices: none -> 9.45 us  [per_device(): lax.all_to_all(jnp.stack([normed] * lax.axis_size('tensor')), 'tensor', 0...]
    ppermute x2, waiting for transfers between devices: 2.64 us -> 11.1 us  [from_behind(): return lax.ppermute(shard, axis, pairs)]
  transfers between devices with their start and end apart: 3 -> 3, of which waited for: 2 -> 2; matrix products, arithmetic and copies ran while one was open for 9% -> 4% of each run, Pallas kernels for 0% -> 0%
where the time goes in v1:
time: 612 us; the launch traced here: 607 us
  waiting for transfers between devices  473 us (77%)
  blocking collectives  37.5 us (6%)
  local copies, waits for them, and re-layouts  35.8 us (6%)
  matrix products  24 us (4%)
  starting transfers between devices  18.1 us (3%)
  other arithmetic  18 us (3%)
    all_to_all x1, waiting for transfers between devices, per_device(): lax.all_to_all(jnp.stack([normed] * lax.axis_size('tensor')), 'tensor', 0...  462 us
    all_to_all x1, blocking collectives, per_device(): lax.all_to_all(gated, 'tensor', split_axis=0, concat_axis=1, tiled=True)  37.5 us
    dot_general x1, matrix products, per_device(): jnp.dot(jnp.concatenate(lax.all_to_all(jnp.stack([normed] * lax.axis_size...  18.2 us
    unnamed x21, local copies, waits for them, and re-layouts  16.5 us
  transfers between devices with their start and end apart: 3, of which 2 were waited for; matrix products, arithmetic and copies ran while one was open for 4% of the time, Pallas kernels for 0%

profile of v1, /device:TPU:70, one launch (start us, length us, event | category | flops | bytes accessed | tf_op | source)
XLA Modules:
  0.0 606.5 jit_solution(12984538366227285616)
XLA Ops:
  0.7 1.5 fusion.6
  2.2 1.6 fusion.8
  3.8 6.0 stack.2
  9.8 9.5 %all-to-all-start = ((bf16[16,128,4096]{2,1,0:T(8,128)(2,1)}), bf16[16,128,4096]{2,1,0:T(8,128)(2,1)}, u32[]{:S(2)}, u32[]{:S(2)}) async-start(bf16[16,128,4096]{2,1,0:T(8,128)(2,1)} %stack.2), calls=%async_computation | async-start | bytes 33554432 | tf_op jit(solution)/shard_map/all_to_all | solution.py:49
  19.2 8.8 %copy.11 = bf16[4096,3,256]{0,2,1:T(8,128)(2,1)} copy(bf16[4096,3,256]{2,0,1:T(8,128)(2,1)} %param.8) | data formatting | bytes 12582912 | tf_op args[2]
  29.3 461.9 %all-to-all-done = bf16[16,128,4096]{2,1,0:T(8,128)(2,1)} async-done(((bf16[16,128,4096]{2,1,0:T(8,128)(2,1)}), bf16[16,128,4096]{2,1,0:T(8,128)(2,1)}, u32[]{:S(2)}, u32[]{:S(2)}) %all-to-all-start) | async-done | bytes 16777248 | tf_op jit(solution)/shard_map/all_to_all | solution.py:49
  491.2 18.2 %convolution_convert_fusion = bf16[2048,768]{1,0:T(8,128)(2,1)S(1)} fusion(bf16[2048,4096]{1,0:T(8,128)(2,1)} %bitcast, bf16[4096,768]{0,1:T(8,128)(2,1)} %bitcast.47), kind=kOutput, calls=%fused_computation.6 | convolution fusion | flops 12886474752 | bytes 26214400 | tf_op jit(solution)/shard_map/dot_general | solution.py:47
  509.4 1.6 copy-done.1
  511.3 1.9 collective-permute-start
  514.4 3.2 copy.12
  517.6 11.1 %collective-permute-done = bf16[2,3,256]{0,2,1:T(8,128)(2,1)S(1)} collective-permute-done((bf16[2,3,256]{0,2,1:T(8,128)(2,1)S(1)}, bf16[2,3,256]{0,2,1:T(8,128)(2,1)S(1)}, u32[]{:S(2)}, u32[]{:S(2)}) %collective-permute-start) | collective-permute-done | bytes 3104 | tf_op jit(solution)/shard_map/ppermute | solution.py:10
  528.6 5.0 select_add_fusion
  533.7 1.9 slice_bitcast_fusion
  535.6 6.7 %collective-permute-start.1 = (bf16[127,256]{0,1:T(8,128)(2,1)S(1)}, bf16[127,256]{0,1:T(8,128)(2,1)S(1)}, u32[]{:S(2)}, u32[]{:S(2)}) collective-permute-start(bf16[127,256]{0,1:T(8,128)(2,1)S(1)} %slice_bitcast_fusion.1), channel_id=1, source_target_pairs={{0,16},{16,32},{32,48},{48,64},{64,80},{80,96},{96,112},{112,128},... | collective-permute-start | bytes 195080 | tf_op jit(solution)/shard_map/ppermute | solution.py:10
  542.3 1.2 broadcast_compare_fusion
  544.3 4.3 broadcast_in_dim.65
  550.2 1.4 copy.27
  551.6 2.0 copy.28
  553.7 1.2 pad_maximum_fusion.1
  554.9 1.5 copy.16
  557.7 5.8 fusion
  564.2 37.5 %all_to_all.15 = bf16[16,128,256]{1,2,0:T(8,128)(2,1)S(1)} all-to-all(bf16[16,128,256]{1,2,0:T(8,128)(2,1)S(1)} %fusion.14), channel_id=1, replica_groups=mesh['context'=16,'tensor'=16] {'tensor'}, dimensions={0} | all-to-all | bytes 2097152 | tf_op jit(solution)/shard_map/all_to_all | solution.py:85
  601.9 1.9 copy.23
  603.8 2.8 fusion.9
  (40 shorter events, 8.1 us)
Async XLA Ops:
  9.8 481.5 %all-to-all-start = ((bf16[16,128,4096]{2,1,0:T(8,128)(2,1)}), bf16[16,128,4096]{2,1,0:T(8,128)(2,1)}, u32[]{:S(2)}, u32[]{:S(2)}) async-start(bf16[16,128,4096]{2,1,0:T(8,128)(2,1)} %stack.2), calls=%async_computation | async-start | bytes 33554432 | tf_op jit(solution)/shard_map/all_to_all | solution.py:49
  19.2 8.8 %copy-start.5 = (bf16[3,3,256]{2,1,0:T(4,128)(2,1)S(1)}, bf16[3,3,256]{2,1,0:T(4,128)(2,1)}, u32[]{:S(2)}) copy-start(bf16[3,3,256]{2,1,0:T(4,128)(2,1)} %param.9) | copy-start | bytes 13828
  19.2 9.4 %copy-start.4 = (s32[2048]{0:T(1024)S(1)}, s32[2048]{0:T(1024)}, u32[]{:S(2)}) copy-start(s32[2048]{0:T(1024)} %param.11) | copy-start | bytes 24580
  509.4 1.6 copy-start.1
  511.3 17.4 %collective-permute-start = (bf16[2,3,256]{0,2,1:T(8,128)(2,1)S(1)}, bf16[2,3,256]{0,2,1:T(8,128)(2,1)S(1)}, u32[]{:S(2)}, u32[]{:S(2)}) collective-permute-start(bf16[2,3,256]{0,2,1:T(8,128)(2,1)S(1)} %bitcast.56), channel_id=1, source_target_pairs={{0,16},{16,32},{32,48},{48,64},{64,80},{80,96},{96,112},{112,128},... | collective-permute-start | bytes 9224 | tf_op jit(solution)/shard_map/ppermute | solution.py:10
  533.6 8.7 %copy-start.3 = (s32[16,128]{1,0:T(8,128)S(1)}, s32[16,128]{1,0:T(8,128)}, u32[]{:S(2)}) copy-start(s32[16,128]{1,0:T(8,128)} %subtract_bitcast_fusion) | copy-start | bytes 24580
  533.6 9.8 %copy-start.6 = (bf16[16,128]{1,0:T(8,128)(2,1)S(1)}, bf16[16,128]{1,0:T(8,128)(2,1)}, u32[]{:S(2)}) copy-start(bf16[16,128]{1,0:T(8,128)(2,1)} %param.10) | copy-start | bytes 12292
  535.6 18.0 %collective-permute-start.1 = (bf16[127,256]{0,1:T(8,128)(2,1)S(1)}, bf16[127,256]{0,1:T(8,128)(2,1)S(1)}, u32[]{:S(2)}, u32[]{:S(2)}) collective-permute-start(bf16[127,256]{0,1:T(8,128)(2,1)S(1)} %slice_bitcast_fusion.1), channel_id=1, source_target_pairs={{0,16},{16,32},{32,48},{48,64},{64,80},{80,96},{96,112},{112,128},... | collective-permute-start | bytes 195080 | tf_op jit(solution)/shard_map/ppermute | solution.py:10
  556.4 1.2 copy-start.2
  601.7 2.1 copy-start
